TPU v7x, 32 devices: a whole 2x2x4 slice. The times are simulated.
32 devices in a mesh: parts: 2 (over y), shard: 2 (over core), blk: 8 (over z, x).
Axes of the slice: x: 2, y: 2, z: 4, core: 2. Of those that a mesh axis runs over, the one named last changes fastest.
Arguments:
- queries_in: bfloat16 [4096, 1024], P(('parts', 'shard', 'blk')), parts along dimension 0, may hold values from -12 to 12
- query_weight: bfloat16 [1024, 1024], replicated, may hold values from -0.1875 to 0.1875
- bank: bfloat16 [2048, 1024], P(('parts', 'shard', 'blk')), parts along dimension 0, may hold values from -110 to 110
- uses: int32 [4096, 2], P(('parts', 'shard', 'blk')), parts along dimension 0, may hold values from 0 to 1, as said below
Outputs:
- retrieved: bfloat16 [4096, 1024], P(('parts', 'shard', 'blk')), parts along dimension 0
There are 2 independent parts, one for each index of `parts`. A program takes and returns all parts, laid end to end along the dimension named above; an argument that names none is the same for every part. Nothing has to cross between parts.
Inputs may be any that keep to these rules, and one draw needn't show every extreme that they name: `uses`: every query lists one or both of the two shards. Of the 128 queries of one device, at most 128 list one shard, and in every draw for every index of blk the queries of both devices at that index all list one same shard.
All inputs are finite; a program needn't handle non-finite values.
Results may differ from a plain program's by a relative error of at most 0.035.
Values may be sent and summed in bfloat16 or wider, within the bound.
A program may use at most 128 MiB of HBM per device.

v0:
```python
import math
import jax
import jax.numpy as jnp
from jax import lax
from jax.sharding import PartitionSpec as P

HEADS = 8
HEAD_DIM = 128
NEGATIVE = -1e30


def local_xla(queries_in, query_weight, bank, uses):
    rows = queries_in.shape[0]
    projected = jnp.dot(queries_in, query_weight, preferred_element_type=jnp.float32).astype(
        jnp.bfloat16
    )
    heads = projected.reshape(rows, HEADS, HEAD_DIM)
    whole = lax.all_gather(bank, ("shard", "blk"), axis=0, tiled=True)
    shard_rows = whole.shape[0] // 2
    chunk_rows = math.gcd(shard_rows, 512)
    chunks = shard_rows // chunk_rows
    blocked = whole.reshape(2, chunks, chunk_rows, HEADS, HEAD_DIM)
    allowed = uses > 0

    def step(carry, keys):
        top_old, total_old, accum_old = carry
        scores = jnp.einsum("thd,srhd->htsr", heads, keys, preferred_element_type=jnp.float32)
        scores = jnp.where(allowed[None, :, :, None], scores * HEAD_DIM ** (-0.5), NEGATIVE)
        top = jnp.maximum(top_old, jnp.max(scores, axis=(2, 3)))
        weights = jnp.exp(scores - top[:, :, None, None])
        factor = jnp.exp(top_old - top)
        total = total_old * factor + jnp.sum(weights, axis=(2, 3))
        accum = accum_old * factor[..., None] + jnp.einsum(
            "htsr,srhd->htd", weights.astype(jnp.bfloat16), keys, preferred_element_type=jnp.float32
        )
        return ((top, total, accum), None)

    start = (
        jnp.full((HEADS, rows), NEGATIVE, jnp.float32),
        jnp.zeros((HEADS, rows), jnp.float32),
        jnp.zeros((HEADS, rows, HEAD_DIM), jnp.float32),
    )
    (top, total, accum), _ = lax.scan(step, start, blocked.transpose(1, 0, 2, 3, 4))
    out = (accum / total[..., None]).astype(jnp.bfloat16)
    return out.transpose(1, 0, 2).reshape(rows, HEADS * HEAD_DIM)


def solution(mesh):
    spec = P(("parts", "shard", "blk"), None)
    return jax.shard_map(
        local_xla, mesh=mesh, in_specs=(spec, P(), spec, spec), out_specs=spec, check_vma=False
    )
```

profile of v0, /device:TPU:0, one launch (start us, length us, event | category | flops | bytes accessed | tf_op | source)
XLA Modules:
  0.0 74.4 jit_solution(16575719060348413938)
XLA Ops:
  6.5 0.0 copy-start
  6.5 0.0 all-gather.2.cloned.1.call-start
  6.5 0.7 all-gather.2.cloned.1.call-update
  7.3 0.9 %copy-done = bf16[1024,1024]{1,0:T(8,128)(2,1)S(1)} copy-done((bf16[1024,1024]{1,0:T(8,128)(2,1)S(1)}, bf16[1024,1024]{1,0:T(8,128)(2,1)}, u32[]{:S(2)}) %copy-start) | copy-done | bytes 2097176
  8.1 1.4 %fusion.15 = bf16[16,8,8,128]{3,1,2,0:T(8,128)(2,1)S(1)} fusion(bf16[128,1024]{1,0:T(8,128)(2,1)} %param.4, bf16[1024,1024]{1,0:T(8,128)(2,1)S(1)} %copy-done), kind=kOutput, calls=%fused_computation.13 | convolution fusion | flops 268566528 | bytes 2621440 | tf_op jit(solution)/shard_map/dot_general | solution.py:14
  9.6 0.7 broadcast_compare_fusion
  10.3 43.4 %all-gather.2.cloned.1.call-done = bf16[1024,1024]{1,0:T(8,128)(2,1)} async-done(((bf16[64,1024]{1,0:T(8,128)(2,1)}), bf16[1024,1024]{1,0:T(8,128)(2,1)}) %all-gather.2.cloned.1.call-update) | async-done | bytes 2097168 | tf_op jit(solution)/shard_map/all_gather | solution.py:18
  53.7 3.6 %copy.17 = bf16[128,8,8,128]{3,2,1,0:T(8,128)(2,1)} copy(bf16[128,8,8,128]{3,1,2,0:T(8,128)(2,1)} %bitcast.31) | data formatting | bytes 4194304
  57.3 4.4 %copy.10 = bf16[2,512,8,128]{1,3,0,2:T(8,128)(2,1)} copy(bf16[2,512,8,128]{3,2,1,0:T(8,128)(2,1)} %bitcast.30) | data formatting | bytes 4194304 | tf_op jit(solution)/shard_map/while/body/jit(dynamic_index_in_dim)/squeeze | solution.py:43
  61.6 0.0 copy-start.1
  61.6 2.6 %fusion = (f32[8,128]{1,0:T(8,128)S(1)}, f32[8,128,2,512]{3,1,2,0:T(8,128)S(1)}) fusion(pred[128,2]{0,1:T(4,128)(4,1)S(1)} %broadcast_compare_fusion, bf16[2,512,8,128]{1,3,0,2:T(8,128)(2,1)} %copy.10, bf16[128,8,128,1]{2,1,0,3:T(8,128)(2,1)S(1)} %bitcast.32), kind=kOutput, calls=%fused_computation.2 | convolution fusion | flops 271580160 | bytes 6557952 | tf_op jit(solution)/shard_map/while/body/eval_jaxpr/thd,srhd->htsr/dot_general | solution.py:27
  64.3 1.1 %fusion.1 = f32[8,128]{1,0:T(8,128)S(1)} fusion(f32[8,128,2,512]{3,1,2,0:T(8,128)S(1)} %get-tuple-element.20, f32[8,128]{1,0:T(8,128)S(1)} %get-tuple-element.18, pred[128,2]{0,1:T(4,128)(4,1)S(1)} %broadcast_compare_fusion), kind=kLoop, calls=%fused_computation.3 | loop fusion | flops 4193280 | bytes 4202752 | tf_op jit(solution)/shard_map/while/body/eval_jaxpr/reduce_sum | solution.py:32
  65.4 0.0 copy-done.1
  65.4 1.3 %fusion.19 = bf16[128,8,128]{0,2,1:T(8,128)(2,1)S(1)} fusion(bf16[2,512,8,128]{1,3,0,2:T(8,128)(2,1)S(1)} %copy-done.1, f32[8,128,2,512]{3,1,2,0:T(8,128)S(1)} %get-tuple-element.20, f32[8,128]{1,0:T(8,128)S(1)} %get-tuple-element.18, pred[128,2]{0,1:T(4,128)(4,1)S(1)} %broadcast_compare_fusion, f32[128,8]{0,1:T(8,128)S(1)} %bitcast_add_fusion, ...), kind=kOutput, calls=%fused_computation.15 | convolution fusion | flops 273022976 | bytes 6566144 | tf_op jit(solution)/shard_map/while/body/eval_jaxpr/htsr,srhd->htd/dot_general | solution.py:33
  66.7 0.9 %copy.11 = bf16[128,1024]{1,0:T(8,128)(2,1)} copy(bf16[128,1024]{0,1:T(8,128)(2,1)S(1)} %bitcast.33) | data formatting | bytes 524288 | tf_op jit(solution)/shard_map/reshape | solution.py:45
  (3 shorter events, 0.1 us)
Async XLA Ops:
  6.5 1.6 %copy-start = (bf16[1024,1024]{1,0:T(8,128)(2,1)S(1)}, bf16[1024,1024]{1,0:T(8,128)(2,1)}, u32[]{:S(2)}) copy-start(bf16[1024,1024]{1,0:T(8,128)(2,1)} %param.5) | copy-start | bytes 6291460
  6.5 47.2 %all-gather.2.cloned.1.call-start = ((), (), s32[]{:S(2)}) async-start(), calls=%async_computation | async-start | bytes 2228224 | tf_op jit(solution)/shard_map/all_gather | solution.py:18
  61.6 3.8 %copy-start.1 = (bf16[2,512,8,128]{1,3,0,2:T(8,128)(2,1)S(1)}, bf16[2,512,8,128]{1,3,0,2:T(8,128)(2,1)}, u32[]{:S(2)}) copy-start(bf16[2,512,8,128]{1,3,0,2:T(8,128)(2,1)} %copy.10) | copy-start | bytes 6291460
Sparse Core Ops, SparseCore 0:
  9.6 44.0 all-gather.1
where the time goes:
time: 74.7 us; the launch traced here: 74.4 us
  waiting for transfers between devices  44.1 us (59%)
  between operations  13.4 us (18%)
  local copies, waits for them, and re-layouts  9.69 us (13%)
  matrix products  5.36 us (7%)
  other arithmetic  1.8 us (2%)
    all_gather x1, waiting for transfers between devices, local_xla(): whole = lax.all_gather(bank, ('shard', 'blk'), axis=0, tiled=True)  43.4 us
    unnamed x6, local copies, waits for them, and re-layouts  4.48 us
    squeeze x1, local copies, waits for them, and re-layouts, local_xla(): lax.scan(step, start, blocked.transpose(1, 0, 2, 3, 4))  4.36 us
    dot_general x1, matrix products, step(): jnp.einsum('thd,srhd->htsr', heads, keys, preferred_element_type=jnp.floa...  2.63 us
  transfers between devices with their start and end apart: 1, of which 1 were waited for; matrix products, arithmetic and copies ran while one was open for 3% of the time, Pallas kernels for 0%

commit v1 on v0

--- a/solution.py
+++ b/solution.py
@@ -9,13 +9,31 @@
 NEGATIVE = -1e30
 
 
+def laid_out(blocks, dim):
+    blocks = jnp.moveaxis(blocks, 0, dim)
+    shape = blocks.shape
+    return blocks.reshape(*shape[:dim], shape[dim] * shape[dim + 1], *shape[dim + 2 :])
+
+
+def collected_by_bits(x, axis):
+    peers = lax.axis_size(axis)
+    pieces = x[None]
+    for level in range(peers.bit_length() - 1):
+        stride = 1 << level
+        other = lax.ppermute(pieces, axis, [(i, i ^ stride) for i in range(peers)])
+        both = jnp.stack([pieces, other])
+        upper = lax.axis_index(axis) >> level & 1
+        pieces = jnp.where(upper == 0, both, both[::-1]).reshape(-1, *x.shape)
+    return pieces
+
+
 def local_xla(queries_in, query_weight, bank, uses):
     rows = queries_in.shape[0]
     projected = jnp.dot(queries_in, query_weight, preferred_element_type=jnp.float32).astype(
         jnp.bfloat16
     )
     heads = projected.reshape(rows, HEADS, HEAD_DIM)
-    whole = lax.all_gather(bank, ("shard", "blk"), axis=0, tiled=True)
+    whole = laid_out(collected_by_bits(bank, ("shard", "blk")), 0)
     shard_rows = whole.shape[0] // 2
     chunk_rows = math.gcd(shard_rows, 512)
     chunks = shard_rows // chunk_rows

time: 74.7 us -> 57.6 us (0.77)
  between operations: 13.4 us -> 0.15 us
  waiting for transfers between devices: 44.1 us -> 33.4 us
  starting transfers between devices: 0.01 us -> 7.49 us
  other arithmetic: 1.8 us -> 4.66 us
  local copies, waits for them, and re-layouts: 9.69 us -> 7.21 us
  matrix products: 5.36 us -> 4.43 us
    all_gather x1 -> x0, waiting for transfers between devices: 43.4 us -> none  [local_xla(): whole = lax.all_gather(bank, ('shard', 'blk'), axis=0, tiled=True)]
    ppermute x0 -> x4, waiting for transfers between devices: none -> 33.4 us  [collected_by_bits(): other = lax.ppermute(pieces, axis, [(i, i ^ stride) for i in range(peers)])]
    ppermute x0 -> x4, starting transfers between devices: none -> 7.49 us  [collected_by_bits(): other = lax.ppermute(pieces, axis, [(i, i ^ stride) for i in range(peers)])]
    another operation x0 -> x5, other arithmetic: none -> 2.56 us  [collected_by_bits(): both = jnp.stack([pieces, other])]
    unnamed x6 -> x10, local copies, waits for them, and re-layouts: 4.48 us -> 2.03 us
    select_n x0 -> x3, other arithmetic: none -> 0.98 us  [collected_by_bits(): pieces = jnp.where(upper == 0, both, both[::-1]).reshape(-1, *x.shape)]
    dot_general x1, matrix products: 1.39 us -> 0.45 us  [local_xla(): jnp.dot(queries_in, query_weight, preferred_element_type=jnp.float32)]
  transfers between devices with their start and end apart: 1 -> 4, of which waited for: 1 -> 4; matrix products, arithmetic and copies ran while one was open for 3% -> 1% of each run, Pallas kernels for 0% -> 0%
where the time goes in v1:
time: 57.6 us; the launch traced here: 57.3 us
  waiting for transfers between devices  33.4 us (58%)
  starting transfers between devices  7.49 us (13%)
  local copies, waits for them, and re-layouts  7.21 us (13%)
  other arithmetic  4.66 us (8%)
  matrix products  4.43 us (8%)
    ppermute x4, waiting for transfers between devices, collected_by_bits(): other = lax.ppermute(pieces, axis, [(i, i ^ stride) for i in range(peers)])  33.4 us
    ppermute x4, starting transfers between devices, collected_by_bits(): other = lax.ppermute(pieces, axis, [(i, i ^ stride) for i in range(peers)])  7.49 us
    squeeze x1, local copies, waits for them, and re-layouts, local_xla(): lax.scan(step, start, blocked.transpose(1, 0, 2, 3, 4))  4.33 us
    dot_general x1, matrix products, step(): jnp.einsum('thd,srhd->htsr', heads, keys, preferred_element_type=jnp.floa...  2.66 us
    another operation x5, other arithmetic, collected_by_bits(): both = jnp.stack([pieces, other])  2.56 us
    unnamed x10, local copies, waits for them, and re-layouts  2.03 us
    dot_general x1, matrix products, step(): jnp.einsum('htsr,srhd->htd', weights.astype(jnp.bfloat16), keys, preferre...  1.33 us
  transfers between devices with their start and end apart: 4, of which 4 were waited for; matrix products, arithmetic and copies ran while one was open for 1% of the time, Pallas kernels for 0%

profile of v1, /device:TPU:0, one launch (start us, length us, event | category | flops | bytes accessed | tf_op | source)
XLA Modules:
  0.0 57.3 jit_solution(2247079728328759645)
XLA Ops:
  0.0 2.9 %collective-permute-start = (bf16[1,64,1024]{2,1,0:T(8,128)(2,1)}, bf16[1,64,1024]{2,1,0:T(8,128)(2,1)S(1)}, u32[]{:S(2)}, u32[]{:S(2)}) collective-permute-start(bf16[1,64,1024]{2,1,0:T(8,128)(2,1)} %bitcast.56), channel_id=1, source_target_pairs={{0,1},{1,0},{2,3},{3,2},{4,5},{5,4},{6,7},{7,6},{8,9},{9,8},{10,11... | collective-permute-start | bytes 393224 | tf_op jit(solution)/shard_map/ppermute | solution.py:23
  2.9 3.7 %collective-permute-done = bf16[1,64,1024]{2,1,0:T(8,128)(2,1)S(1)} collective-permute-done((bf16[1,64,1024]{2,1,0:T(8,128)(2,1)}, bf16[1,64,1024]{2,1,0:T(8,128)(2,1)S(1)}, u32[]{:S(2)}, u32[]{:S(2)}) %collective-permute-start) | collective-permute-done | bytes 131104 | tf_op jit(solution)/shard_map/ppermute | solution.py:23
  6.6 0.9 %pad_maximum_fusion.3 = bf16[2,1,64,1024]{3,2,1,0:T(8,128)(2,1)S(1)} fusion(bf16[1,1,64,1024]{3,2,1,0:T(8,128)(2,1)S(1)} %bitcast.58, bf16[1,1,64,1024]{3,2,1,0:T(8,128)(2,1)} %bitcast.57), kind=kLoop, calls=%fused_computation.23 | loop fusion | flops 131072 | bytes 524288 | tf_op jit(solution)/shard_map/stack | solution.py:24
  7.6 0.1 fusion.25
  7.7 1.9 %collective-permute-start.1 = (bf16[2,64,1024]{2,1,0:T(8,128)(2,1)S(1)}, bf16[2,64,1024]{2,1,0:T(8,128)(2,1)S(1)}, u32[]{:S(2)}, u32[]{:S(2)}) collective-permute-start(bf16[2,64,1024]{2,1,0:T(8,128)(2,1)S(1)} %get-tuple-element.18), channel_id=1, source_target_pairs={{0,2},{1,3},{2,0},{3,1},{4,6},{5,7},{6,4},{7,5},{8,10},{9,11},{10,... | collective-permute-start | bytes 786440 | tf_op jit(solution)/shard_map/ppermute | solution.py:23
  9.6 5.7 %collective-permute-done.1 = bf16[2,64,1024]{2,1,0:T(8,128)(2,1)S(1)} collective-permute-done((bf16[2,64,1024]{2,1,0:T(8,128)(2,1)S(1)}, bf16[2,64,1024]{2,1,0:T(8,128)(2,1)S(1)}, u32[]{:S(2)}, u32[]{:S(2)}) %collective-permute-start.1) | collective-permute-done | bytes 262176 | tf_op jit(solution)/shard_map/ppermute | solution.py:23
  15.2 0.1 pad_maximum_fusion.2
  15.3 0.0 copy-start.3
  15.3 0.1 reverse_select_fusion.2
  15.4 2.6 %collective-permute-start.2 = (bf16[4,64,1024]{2,1,0:T(8,128)(2,1)S(1)}, bf16[4,64,1024]{2,1,0:T(8,128)(2,1)S(1)}, u32[]{:S(2)}, u32[]{:S(2)}) collective-permute-start(bf16[4,64,1024]{2,1,0:T(8,128)(2,1)S(1)} %bitcast.50), channel_id=1, source_target_pairs={{0,4},{1,5},{2,6},{3,7},{4,0},{5,1},{6,2},{7,3},{8,12},{9,13},{10,... | collective-permute-start | bytes 1572872 | tf_op jit(solution)/shard_map/ppermute | solution.py:23
  18.0 21.8 %collective-permute-done.2 = bf16[4,64,1024]{2,1,0:T(8,128)(2,1)S(1)} collective-permute-done((bf16[4,64,1024]{2,1,0:T(8,128)(2,1)S(1)}, bf16[4,64,1024]{2,1,0:T(8,128)(2,1)S(1)}, u32[]{:S(2)}, u32[]{:S(2)}) %collective-permute-start.2) | collective-permute-done | bytes 524320 | tf_op jit(solution)/shard_map/ppermute | solution.py:23
  39.8 0.1 pad_maximum_fusion.1
  39.9 0.3 reverse_select_fusion.1
  40.2 0.1 collective-permute-start.3
  40.3 0.4 fusion.15
  40.8 2.2 %collective-permute-done.3 = bf16[8,64,1024]{2,1,0:T(8,128)(2,1)} collective-permute-done((bf16[8,64,1024]{2,1,0:T(8,128)(2,1)S(1)}, bf16[8,64,1024]{2,1,0:T(8,128)(2,1)}, u32[]{:S(2)}, u32[]{:S(2)}) %collective-permute-start.3) | collective-permute-done | bytes 1048608 | tf_op jit(solution)/shard_map/ppermute | solution.py:23
  43.0 1.4 %pad_maximum_fusion = bf16[2,8,64,1024]{3,2,1,0:T(8,128)(2,1)S(1)} fusion(bf16[1,8,64,1024]{3,2,1,0:T(8,128)(2,1)} %bitcast.12, bf16[1,8,64,1024]{3,2,1,0:T(8,128)(2,1)S(1)} %bitcast.49), kind=kLoop, calls=%fused_computation.7 | loop fusion | flops 1048576 | bytes 4194304 | tf_op jit(solution)/shard_map/stack | solution.py:24
  44.4 0.6 %reverse_select_fusion = bf16[2,8,64,1024]{3,2,1,0:T(8,128)(2,1)S(1)} fusion(bf16[2,8,64,1024]{3,2,1,0:T(8,128)(2,1)S(1)} %pad_maximum_fusion, pred[]{:T(512)S(6)} %eq.12), kind=kLoop, calls=%fused_computation.5 | loop fusion | flops 1048576 | bytes 4194305 | tf_op jit(solution)/shard_map/jit(_where)/select_n | solution.py:26
  45.1 2.0 %copy.17 = bf16[128,8,8,128]{3,2,1,0:T(8,128)(2,1)} copy(bf16[128,8,8,128]{3,1,2,0:T(8,128)(2,1)S(1)} %bitcast.46) | data formatting | bytes 4194304
  47.0 4.3 %copy.10 = bf16[2,512,8,128]{1,3,0,2:T(8,128)(2,1)} copy(bf16[2,512,8,128]{3,2,1,0:T(8,128)(2,1)} %bitcast.47) | data formatting | bytes 4194304 | tf_op jit(solution)/shard_map/while/body/jit(dynamic_index_in_dim)/squeeze | solution.py:61
  51.4 2.7 %fusion = (f32[8,128]{1,0:T(8,128)S(1)}, f32[8,128,2,512]{3,1,2,0:T(8,128)S(1)}) fusion(pred[128,2]{0,1:T(4,128)(4,1)S(1)} %broadcast_compare_fusion, bf16[2,512,8,128]{1,3,0,2:T(8,128)(2,1)} %copy.10, bf16[128,8,128,1]{2,1,0,3:T(8,128)(2,1)S(1)} %bitcast.52), kind=kOutput, calls=%fused_computation.2 | convolution fusion | flops 271580160 | bytes 6557952 | tf_op jit(solution)/shard_map/while/body/eval_jaxpr/thd,srhd->htsr/dot_general | solution.py:45
  54.0 1.1 %fusion.1 = f32[8,128]{1,0:T(8,128)S(1)} fusion(f32[8,128,2,512]{3,1,2,0:T(8,128)S(1)} %get-tuple-element.30, f32[8,128]{1,0:T(8,128)S(1)} %get-tuple-element.20, pred[128,2]{0,1:T(4,128)(4,1)S(1)} %broadcast_compare_fusion), kind=kLoop, calls=%fused_computation.3 | loop fusion | flops 4193280 | bytes 4202752 | tf_op jit(solution)/shard_map/while/body/eval_jaxpr/reduce_sum | solution.py:50
  55.1 1.3 %fusion.19 = bf16[128,8,128]{0,2,1:T(8,128)(2,1)S(1)} fusion(bf16[2,512,8,128]{1,3,0,2:T(8,128)(2,1)S(1)} %copy-done.1, f32[8,128,2,512]{3,1,2,0:T(8,128)S(1)} %get-tuple-element.30, f32[8,128]{1,0:T(8,128)S(1)} %get-tuple-element.20, pred[128,2]{0,1:T(4,128)(4,1)S(1)} %broadcast_compare_fusion, f32[128,8]{0,1:T(8,128)S(1)} %bitcast_add_fusion, ...), kind=kOutput, calls=%fused_computation.19 | convolution fusion | flops 273022976 | bytes 6566144 | tf_op jit(solution)/shard_map/while/body/eval_jaxpr/htsr,srhd->htd/dot_general | solution.py:51
  56.5 0.9 %copy.11 = bf16[128,1024]{1,0:T(8,128)(2,1)} copy(bf16[128,1024]{0,1:T(8,128)(2,1)S(1)} %bitcast.54) | data formatting | bytes 524288 | tf_op jit(solution)/shard_map/reshape | solution.py:63
  (11 shorter events, 0.1 us)
Async XLA Ops:
  0.0 40.3 %copy-start = (bf16[1024,1024]{1,0:T(8,128)(2,1)S(1)}, bf16[1024,1024]{1,0:T(8,128)(2,1)}, u32[]{:S(2)}) copy-start(bf16[1024,1024]{1,0:T(8,128)(2,1)} %param.5) | copy-start | bytes 6291460
  0.0 40.3 %copy-start.2 = (bf16[128,1024]{1,0:T(8,128)(2,1)S(1)}, bf16[128,1024]{1,0:T(8,128)(2,1)}, u32[]{:S(2)}) copy-start(bf16[128,1024]{1,0:T(8,128)(2,1)} %param.4) | copy-start | bytes 786436
  0.0 6.6 %collective-permute-start = (bf16[1,64,1024]{2,1,0:T(8,128)(2,1)}, bf16[1,64,1024]{2,1,0:T(8,128)(2,1)S(1)}, u32[]{:S(2)}, u32[]{:S(2)}) collective-permute-start(bf16[1,64,1024]{2,1,0:T(8,128)(2,1)} %bitcast.56), channel_id=1, source_target_pairs={{0,1},{1,0},{2,3},{3,2},{4,5},{5,4},{6,7},{7,6},{8,9},{9,8},{10,11... | collective-permute-start | bytes 393224 | tf_op jit(solution)/shard_map/ppermute | solution.py:23
  7.7 7.6 %collective-permute-start.1 = (bf16[2,64,1024]{2,1,0:T(8,128)(2,1)S(1)}, bf16[2,64,1024]{2,1,0:T(8,128)(2,1)S(1)}, u32[]{:S(2)}, u32[]{:S(2)}) collective-permute-start(bf16[2,64,1024]{2,1,0:T(8,128)(2,1)S(1)} %get-tuple-element.18), channel_id=1, source_target_pairs={{0,2},{1,3},{2,0},{3,1},{4,6},{5,7},{6,4},{7,5},{8,10},{9,11},{10,... | collective-permute-start | bytes 786440 | tf_op jit(solution)/shard_map/ppermute | solution.py:23
  15.3 25.5 %copy-start.3 = (s32[128,2]{0,1:T(2,128)S(1)}, s32[128,2]{0,1:T(2,128)}, u32[]{:S(2)}) copy-start(s32[128,2]{0,1:T(2,128)} %param.7) | copy-start | bytes 3076
  15.4 24.4 %collective-permute-start.2 = (bf16[4,64,1024]{2,1,0:T(8,128)(2,1)S(1)}, bf16[4,64,1024]{2,1,0:T(8,128)(2,1)S(1)}, u32[]{:S(2)}, u32[]{:S(2)}) collective-permute-start(bf16[4,64,1024]{2,1,0:T(8,128)(2,1)S(1)} %bitcast.50), channel_id=1, source_target_pairs={{0,4},{1,5},{2,6},{3,7},{4,0},{5,1},{6,2},{7,3},{8,12},{9,13},{10,... | collective-permute-start | bytes 1572872 | tf_op jit(solution)/shard_map/ppermute | solution.py:23
  40.2 2.9 %collective-permute-start.3 = (bf16[8,64,1024]{2,1,0:T(8,128)(2,1)S(1)}, bf16[8,64,1024]{2,1,0:T(8,128)(2,1)}, u32[]{:S(2)}, u32[]{:S(2)}) collective-permute-start(bf16[8,64,1024]{2,1,0:T(8,128)(2,1)S(1)} %bitcast.48), channel_id=1, source_target_pairs={{0,8},{1,9},{2,10},{3,11},{4,12},{5,13},{6,14},{7,15},{8,0},{9,1},... | collective-permute-start | bytes 3145736 | tf_op jit(solution)/shard_map/ppermute | solution.py:23
  51.4 3.8 %copy-start.1 = (bf16[2,512,8,128]{1,3,0,2:T(8,128)(2,1)S(1)}, bf16[2,512,8,128]{1,3,0,2:T(8,128)(2,1)}, u32[]{:S(2)}) copy-start(bf16[2,512,8,128]{1,3,0,2:T(8,128)(2,1)} %copy.10) | copy-start | bytes 6291460
